TPU v7x, 1024 devices: a whole 4x4x32 slice. The times are simulated.
1024 devices in a mesh: group: 4 (over x), ingroup: 8 (over y, core), hid: 32 (over z).
Axes of the slice: x: 4, y: 4, z: 32, core: 2. Of those that a mesh axis runs over, the one named last changes fastest.
Arguments:
- tokens: bfloat16 [2048, 2048], P(('group', 'hid')), may hold values from -6 to 6
- grad_mixed: bfloat16 [2048, 2048], P(('group', 'hid')), may hold values from -6 to 6
- expert_ids: int32 [2048, 6], P(('group', 'hid')), may hold values from 0 to 63, all different within a row; in each aligned block of 16 rows (0 to 15, 16 to 31, ...) at most 2 rows name the same one
- gate_weight: float32 [2048, 6], P(('group', 'hid')), may hold values from 0.05 to 1
- w_gate: bfloat16 [64, 2048, 1408], P('hid', None, 'ingroup'), may hold values from -0.125 to 0.125
- w_up: bfloat16 [64, 2048, 1408], P('hid', None, 'ingroup'), may hold values from -0.125 to 0.125
- w_down: bfloat16 [64, 1408, 2048], P('hid', 'ingroup'), may hold values from -0.15625 to 0.15625
Outputs:
- mixed: bfloat16 [2048, 2048], P(('group', 'hid'), 'ingroup')
- grad_tokens: bfloat16 [2048, 2048], P(('group', 'hid'), 'ingroup')
- grad_gate: float32 [64, 2048, 1408], P('hid', 'group', 'ingroup')
- grad_up: float32 [64, 2048, 1408], P('hid', 'group', 'ingroup')
- grad_down: float32 [64, 1408, 2048], P('hid', 'ingroup', 'group')
Inputs may be any that keep to these rules, and one draw needn't show every extreme that they name: `expert_ids`: each row names 6 different experts. Among the 16 tokens of one index of group and hid (aligned blocks of rows), no expert is named more than 2 times, and that bound is reached.
All inputs are finite; a program needn't handle non-finite values.
Results may differ from a plain program's by a relative error of at most 0.015.
Values may be sent and summed in bfloat16 or wider, within the bound.
A program may use at most 32 MiB of HBM per device.

v0:
```python
import jax
import jax.numpy as jnp
from jax import lax
from jax.sharding import PartitionSpec as P

TOP = 6


def sent_together(arrays, axis, split_dim, concat_dim, along):
    widths = [a.shape[along] for a in arrays]
    both = jnp.concatenate(arrays, axis=along)
    result = lax.all_to_all(both, axis, split_axis=split_dim, concat_axis=concat_dim, tiled=True)
    return tuple(jnp.split(result, [sum(widths[:k]) for k in range(1, len(widths))], axis=along))


def sent_together_2(arrays, axis, dim, along):
    widths = [a.shape[along] for a in arrays]
    both = jnp.concatenate(arrays, axis=along)
    result = lax.all_gather(both, axis, axis=dim, tiled=True)
    return tuple(jnp.split(result, [sum(widths[:k]) for k in range(1, len(widths))], axis=along))


def side_by_side(arrays, axis, dim, along):
    both = jnp.concatenate(arrays, axis=along)
    result, at, outs = (lax.psum_scatter(both, axis, scatter_dimension=dim, tiled=True), 0, [])
    for a in arrays:
        outs.append(lax.slice_in_dim(result, at, at + a.shape[along], axis=along))
        at += a.shape[along]
    return tuple(outs)


def in_blocks(value, dim, length):
    dims = value.shape
    pieces = value.reshape(*dims[:dim], length, dims[dim] // length, *dims[dim + 1 :])
    return jnp.moveaxis(pieces, dim, 0)


def summed_on_arrival(value, axis, dim):
    pieces = in_blocks(value, dim, lax.axis_size(axis))
    arrived = lax.all_to_all(pieces, axis, split_axis=0, concat_axis=0, tiled=True)
    return arrived.astype(jnp.float32).sum(axis=0)


def side_by_side_2(arrays, axis, dim, along):
    ends, at = ([], 0)
    for a in arrays[:-1]:
        at += a.shape[along]
        ends.append(at)
    both = jnp.concatenate(arrays, axis=along)
    return tuple(jnp.split(summed_on_arrival(both, axis, dim), ends, axis=along))


def shards(tokens, grad_mixed, expert_ids, gate_weight, w_gate, w_up, w_down):
    tok_count = tokens.shape[0]
    width = tokens.shape[1]
    n_hid = lax.axis_size("hid")
    exp_dev = w_gate.shape[0]
    experts_all = exp_dev * n_hid
    capacity = tok_count // 8
    slots_total = experts_all * capacity
    flat = expert_ids.reshape(tok_count * TOP)
    onehot = (flat[:, None] == jnp.arange(experts_all, dtype=jnp.int32)[None, :]).astype(jnp.int32)
    rank = jnp.sum((jnp.cumsum(onehot, axis=0) - onehot) * onehot, axis=1)
    owner_idx = flat // exp_dev
    local_idx = flat % exp_dev
    slot = (local_idx * n_hid + owner_idx) * capacity + rank
    token_index = jnp.arange(tok_count * TOP, dtype=jnp.int32) // TOP
    token_of = jnp.zeros((slots_total,), jnp.int32).at[slot].set(token_index)
    live_of = jnp.zeros((slots_total,), jnp.bool_).at[slot].set(True)
    gate_of = (
        jnp.zeros((slots_total,), jnp.float32).at[slot].set(gate_weight.reshape(tok_count * TOP))
    )
    part_width = width // lax.axis_size("ingroup")
    start = lax.axis_index("ingroup") * part_width
    tok_part = lax.dynamic_slice_in_dim(tokens, start, part_width, 1)
    grad_part = lax.dynamic_slice_in_dim(grad_mixed, start, part_width, 1)
    send_x = jnp.where(live_of[:, None], tok_part[token_of], jnp.zeros((), jnp.bfloat16))
    send_g = (gate_of[:, None] * grad_part[token_of].astype(jnp.float32)).astype(jnp.bfloat16)
    shape_part = (exp_dev, n_hid, capacity, part_width)
    part_x, part_g = sent_together(
        (send_x.reshape(shape_part), send_g.reshape(shape_part)), "hid", 1, 1, 0
    )
    recv_x, recv_g = sent_together_2((part_x, part_g), "ingroup", 3, 0)
    rows = n_hid * capacity
    x_rows = recv_x.reshape(exp_dev, rows, width)
    gated = recv_g.reshape(exp_dev, rows, width)
    gate_pre = jnp.einsum("emd,edh->emh", x_rows, w_gate, preferred_element_type=jnp.float32)
    up_pre = jnp.einsum("emd,edh->emh", x_rows, w_up, preferred_element_type=jnp.float32)
    sigmoid_gate = jax.nn.sigmoid(gate_pre)
    silu = gate_pre * sigmoid_gate
    hidden = (silu * up_pre).astype(jnp.bfloat16)
    out_part = jnp.einsum("emh,ehd->emd", hidden, w_down, preferred_element_type=jnp.float32)
    d_hidden = jnp.einsum("emd,ehd->emh", gated, w_down, preferred_element_type=jnp.float32)
    d_up = (d_hidden * silu).astype(jnp.bfloat16)
    d_gate = (d_hidden * up_pre * sigmoid_gate * (1.0 + gate_pre * (1.0 - sigmoid_gate))).astype(
        jnp.bfloat16
    )
    term_down = jnp.einsum("emh,emd->ehd", hidden, gated, preferred_element_type=jnp.float32)
    term_gate = jnp.einsum("emd,emh->edh", x_rows, d_gate, preferred_element_type=jnp.float32)
    term_up = jnp.einsum("emd,emh->edh", x_rows, d_up, preferred_element_type=jnp.float32)
    in_part = jnp.einsum("emh,edh->emd", d_gate, w_gate, preferred_element_type=jnp.float32)
    in_part = in_part + jnp.einsum("emh,edh->emd", d_up, w_up, preferred_element_type=jnp.float32)
    grad_gate, grad_up, grad_down = (
        *tuple(
            (
                part.astype(jnp.float32)
                for part in side_by_side(
                    (term_gate.astype(jnp.bfloat16), term_up.astype(jnp.bfloat16)), "group", 1, 0
                )
            )
        ),
        lax.psum_scatter(
            term_down.astype(jnp.bfloat16), "group", scatter_dimension=2, tiled=True
        ).astype(jnp.float32),
    )
    out_share, in_share = side_by_side_2(
        (out_part.astype(jnp.bfloat16), in_part.astype(jnp.bfloat16)), "ingroup", 2, 0
    )
    narrow = out_share.shape[2]
    out_share = out_share.astype(jnp.bfloat16)
    in_share = in_share.astype(jnp.bfloat16)
    back_shape = (exp_dev, n_hid, capacity, narrow)
    home_out, home_in = sent_together(
        (out_share.reshape(back_shape), in_share.reshape(back_shape)), "hid", 1, 1, 0
    )
    picked_out = home_out.reshape(slots_total, narrow)[slot].reshape(tok_count, TOP, narrow)
    picked_in = home_in.reshape(slots_total, narrow)[slot].reshape(tok_count, TOP, narrow)
    mixed = jnp.sum(gate_weight[:, :, None] * picked_out.astype(jnp.float32), axis=1).astype(
        jnp.bfloat16
    )
    grad_tokens = jnp.sum(picked_in.astype(jnp.float32), axis=1).astype(jnp.bfloat16)
    return (mixed, grad_tokens, grad_gate, grad_up, grad_down)


def solution(mesh):
    placed = (
        P(("group", "hid"), None),
        P(("group", "hid"), None),
        P(("group", "hid"), None),
        P(("group", "hid"), None),
        P("hid", None, "ingroup"),
        P("hid", None, "ingroup"),
        P("hid", "ingroup", None),
    )
    return jax.shard_map(
        shards,
        mesh=mesh,
        in_specs=placed,
        out_specs=(
            P(("group", "hid"), "ingroup"),
            P(("group", "hid"), "ingroup"),
            P("hid", "group", "ingroup"),
            P("hid", "group", "ingroup"),
            P("hid", "ingroup", "group"),
        ),
        check_vma=False,
    )
```

profile of v0, /device:TPU:1, one launch (start us, length us, event | category | flops | bytes accessed | tf_op | source)
XLA Modules:
  0.0 224.4 jit_solution(2151472179275641457)
XLA Ops:
  7.2 0.9 copy.79
  8.4 0.1 reduce_window_sum.11
  8.5 0.2 select_reduce_fusion
  8.7 0.9 scatter_custom_fusion.1
  9.6 0.7 constant_dynamic-slice_fusion
  10.4 0.8 gather_fusion.1
  11.3 0.8 copy.78
  12.1 0.9 scatter_custom_fusion.2
  13.0 0.1 mul.76
  13.2 0.9 gather_fusion
  14.1 0.9 scatter_custom_fusion
  15.1 0.1 broadcast_in_dim.38
  15.5 0.1 copy.86
  15.7 58.8 %all_to_all.15 = bf16[4,32,2,256]{3,2,0,1:T(2,128)(2,1)} all-to-all(bf16[4,32,2,256]{3,2,0,1:T(2,128)(2,1)S(1)} %copy.86), channel_id=1, replica_groups=mesh['group'=4,'ingroup'=8,'hid'=32] {'hid'}, dimensions={1} | all-to-all | bytes 262144 | tf_op jit(solution)/shard_map/all_to_all | solution.py:12
  74.6 25.1 %all-gather.2.cloned.1.call-done = bf16[4,32,2,2048]{3,2,0,1:T(2,128)(2,1)} async-done(((bf16[4,32,2,256]{3,2,0,1:T(2,128)(2,1)}), bf16[4,32,2,2048]{3,2,0,1:T(2,128)(2,1)}) %all-gather.2.cloned.1.call-update) | async-done | bytes 1048592 | tf_op jit(solution)/shard_map/all_gather | solution.py:19
  99.6 2.8 %fusion.13 = (bf16[2,32,2,2048]{3,2,0,1:T(2,128)(2,1)}, bf16[2,32,2,2048]{3,2,0,1:T(2,128)(2,1)S(1)}) fusion(bf16[4,32,2,2048]{3,2,0,1:T(2,128)(2,1)} %all-gather.2.cloned.1.call-done), kind=kLoop, calls=%fused_computation.57 | loop fusion | bytes 2097152 | tf_op jit(solution)/shard_map/split | solution.py:20
  102.4 1.2 copy.87
  103.6 1.3 reshape.185
  104.9 2.2 copy.88
  107.1 2.0 reshape.186
  109.2 0.6 fusion.16
  109.8 0.8 copy-done.2
  110.5 0.1 copy-done.3
  110.6 0.6 fusion.17
  111.2 0.6 multiply_convert_fusion.2
  111.9 0.6 copy-done.4
  112.5 1.7 convolution_convert_fusion
  114.2 0.6 convolution_convert_fusion.1
  114.8 0.6 convolution_convert_fusion.2
  115.4 1.8 pad_maximum_fusion
  117.2 0.8 copy-done.5
  118.1 1.7 convolution_convert_fusion.3
  119.8 0.4 fusion.18
  120.2 0.4 fusion
  120.7 0.1 copy.101
  120.8 19.1 %all_to_all.16 = bf16[8,4,64,256]{3,2,1,0:T(8,128)(2,1)S(1)} all-to-all(bf16[8,4,64,256]{3,2,1,0:T(8,128)(2,1)S(1)} %bitcast.34), channel_id=1, replica_groups=mesh['group'=4,'ingroup'=8,'hid'=32] {'ingroup'}, dimensions={0} | all-to-all | bytes 2097152 | tf_op jit(solution)/shard_map/all_to_all | solution.py:40
  139.9 0.1 reduce.1
  140.2 0.1 pad_maximum_fusion.3
  140.4 0.8 copy.92
  141.1 22.6 %all-to-all-start.2 = ((bf16[4,32,2,256]{3,2,0,1:T(2,128)(2,1)}), bf16[4,32,2,256]{3,2,0,1:T(2,128)(2,1)S(1)}, u32[]{:S(2)}, u32[]{:S(2)}) async-start(bf16[4,32,2,256]{3,2,0,1:T(2,128)(2,1)} %copy.92), calls=%async_computation.2 | async-start | bytes 262144 | tf_op jit(solution)/shard_map/all_to_all | solution.py:12
  163.8 29.3 %all-to-all-done.2 = bf16[4,32,2,256]{3,2,0,1:T(2,128)(2,1)S(1)} async-done(((bf16[4,32,2,256]{3,2,0,1:T(2,128)(2,1)}), bf16[4,32,2,256]{3,2,0,1:T(2,128)(2,1)S(1)}, u32[]{:S(2)}, u32[]{:S(2)}) %all-to-all-start.2) | async-done | bytes 131104 | tf_op jit(solution)/shard_map/all_to_all | solution.py:12
  193.3 0.8 gather_fusion.2
  194.2 0.8 gather_fusion.3
  195.0 0.6 reduce_sum.45
  195.6 0.7 multiply_reduce_fusion
  196.3 1.9 convert_element_type.81
  198.2 17.2 %reduce-scatter.3.cloned.1.call-done = bf16[4,512,176]{1,2,0:T(8,128)(2,1)} async-done(((bf16[4,2048,176]{1,2,0:T(8,128)(2,1)}), bf16[4,512,176]{1,2,0:T(8,128)(2,1)}) %reduce-scatter.3.cloned.1.call-update) | async-done | bytes 720912 | tf_op jit(solution)/shard_map/reduce_scatter | solution.py:25
  215.5 2.4 %slice_convert_fusion = (f32[2,512,176]{1,2,0:T(8,128)}, f32[2,512,176]{1,2,0:T(8,128)}) fusion(bf16[4,512,176]{1,2,0:T(8,128)(2,1)} %reduce-scatter.3.cloned.1.call-done), kind=kLoop, calls=%fused_computation.16 | loop fusion | flops 360448 | bytes 2162688 | tf_op jit(solution)/shard_map/convert_element_type | solution.py:106
  (43 shorter events, 1.6 us)
Async XLA Ops:
  7.2 104.1 %copy-start = (bf16[2,2048,176]{1,2,0:T(8,128)(2,1)S(1)}, bf16[2,2048,176]{1,2,0:T(8,128)(2,1)}, u32[]{:S(2)}) copy-start(bf16[2,2048,176]{1,2,0:T(8,128)(2,1)} %param.12) | copy-start | bytes 4325380
  7.2 92.4 %all-gather.2.cloned.1.call-start = ((), (), s32[]{:S(2)}) async-start(), calls=%async_computation.5 | async-start | bytes 1179648 | tf_op jit(solution)/shard_map/all_gather | solution.py:19
  74.5 121.8 %reduce-scatter.5.cloned.1.call-start = ((), (), s32[]{:S(2)}) async-start(), calls=%async_computation.7 | async-start | bytes 1802240 | tf_op jit(solution)/shard_map/reduce_scatter | solution.py:112
  103.6 5.6 %copy-start.1 = (bf16[2,2048,176]{1,2,0:T(8,128)(2,1)S(1)}, bf16[2,2048,176]{1,2,0:T(8,128)(2,1)}, u32[]{:S(2)}) copy-start(bf16[2,2048,176]{1,2,0:T(8,128)(2,1)} %param.11) | copy-start | bytes 4325380
  109.2 1.4 copy-start.2
  109.2 1.5 copy-start.3
  111.8 0.6 copy-start.4
  114.2 101.3 %reduce-scatter.3.cloned.1.call-start = ((), (), s32[]{:S(2)}) async-start(), calls=%async_computation.6 | async-start | bytes 3604480 | tf_op jit(solution)/shard_map/reduce_scatter | solution.py:25
  117.2 0.8 copy-start.5
  141.1 51.9 %all-to-all-start.2 = ((bf16[4,32,2,256]{3,2,0,1:T(2,128)(2,1)}), bf16[4,32,2,256]{3,2,0,1:T(2,128)(2,1)S(1)}, u32[]{:S(2)}, u32[]{:S(2)}) async-start(bf16[4,32,2,256]{3,2,0,1:T(2,128)(2,1)} %copy.92), calls=%async_computation.2 | async-start | bytes 262144 | tf_op jit(solution)/shard_map/all_to_all | solution.py:12
Sparse Core Ops, SparseCore 0:
  74.6 24.9 all-gather.1
  114.3 42.7 reduce-scatter.4
  160.6 54.8 reduce-scatter.2
where the time goes:
time: 225 us; the launch traced here: 224 us
  blocking collectives  77.9 us (35%)
  waiting for transfers between devices  71.6 us (32%)
  starting transfers between devices  22.8 us (10%)
  local copies, waits for them, and re-layouts  22.4 us (10%)
  between operations  14.1 us (6%)
  other arithmetic  8.51 us (4%)
  matrix products  7.14 us (3%)
    all_to_all x1, blocking collectives, sent_together(): lax.all_to_all(both, axis, split_axis=split_dim, concat_axis=concat_dim,...  58.8 us
    all_to_all x1, waiting for transfers between devices, sent_together(): lax.all_to_all(both, axis, split_axis=split_dim, concat_axis=concat_dim,...  29.3 us
    all_gather x1, waiting for transfers between devices, sent_together_2(): result = lax.all_gather(both, axis, axis=dim, tiled=True)  25.1 us
    all_to_all x1, starting transfers between devices, sent_together(): lax.all_to_all(both, axis, split_axis=split_dim, concat_axis=concat_dim,...  22.6 us
    all_to_all x1, blocking collectives, summed_on_arrival(): lax.all_to_all(pieces, axis, split_axis=0, concat_axis=0, tiled=True)  19.1 us
    reduce_scatter x1, waiting for transfers between devices, side_by_side(): lax.psum_scatter(both, axis, scatter_dimension=dim, tiled=True)  17.2 us
    split x3, local copies, waits for them, and re-layouts, sent_together_2(): jnp.split(result, [sum(widths[:k]) for k in range(1, len(widths))], axis=...  6.15 us
  transfers between devices with their start and end apart: 4, of which 3 were waited for; matrix products, arithmetic and copies ran while one was open for 5% of the time, Pallas kernels for 0%

commit v1 on v0

v1 whole, which is shorter than its diff:
```python
import functools

import jax
import jax.numpy as jnp
from jax import lax
from jax.experimental import pallas as pl
from jax.experimental.pallas import tpu as pltpu
from jax.sharding import PartitionSpec as P

MESH = pl.DeviceIdType.MESH
BF = jnp.bfloat16
F32 = jnp.float32
CAP = 2
LANES = 128

NN = (((1,), (0,)), ((), ()))
NT = (((1,), (1,)), ((), ()))
TN = (((0,), (0,)), ((), ()))


def dot(a, b, dims=NN):
    return lax.dot_general(a, b, dims, preferred_element_type=F32)


def iota(shape, dim):
    return lax.broadcasted_iota(jnp.int32, shape, dim)


def kernel(
    dims,
    ids_ref, gw_ref, tok_hbm, grd_hbm, wg_hbm, wu_hbm, wd_hbm,
    mixed_ref, gtok_ref, gg_hbm, gu_hbm, gd_hbm,
    tok, grd, wg, wu, wd, sel, unperm, perm,
    tile_s, tile_r, acts, part_s, part_r, back_s, back_r,
    xg_r, hr, og, ou, od,
    in_sem, out_sem, send_sem, z_sem, y_sem, rs_sem, zb_sem, xg_sem, hr_sem,
):
    n_g, n_j, n_h, chunks, depth, per, top = dims
    rows = depth * CAP
    half = depth // 2
    toks = ids_ref.shape[0]
    g, j, h = lax.axis_index("group"), lax.axis_index("ingroup"), lax.axis_index("hid")
    width = 2 * LANES

    lanes = pl.ds(pl.multiple_of(j * width, width), width)
    loads = [
        pltpu.make_async_copy(src, dst, in_sem.at[n])
        for n, (src, dst) in enumerate(
            (
                (tok_hbm.at[:, lanes], tok),
                (grd_hbm.at[:, lanes], grd),
                (wg_hbm, wg),
                (wu_hbm, wu),
                (wd_hbm, wd),
            )
        )
    ]
    for load in loads:
        load.start()

    barrier = pltpu.get_barrier_semaphore()

    def greet(count, device):
        def body(o, carry):
            pl.semaphore_signal(
                barrier, inc=1, device_id=device(o), device_id_type=MESH
            )
            return carry

        lax.fori_loop(1, count, body, 0)

    def hid_peer(o):
        return (g, j, lax.rem(h + o, n_h))

    def in_peer(o):
        return (g, lax.rem(j + o, n_j), h)

    def group_peer(o):
        return (lax.rem(g + o, n_g), j, h)

    greet(n_h, hid_peer)
    greet(n_j, in_peer)
    greet(n_g, group_peer)

    total = n_h * 16
    lane = iota((1, total), 1)
    pos = lane // 16
    which, part = (lane // 8) % 2, (lane // 4) % 2
    expert_local, place = (lane // 2) % 2, lane % 2
    ck, i = pos // depth, pos % depth
    delta = jnp.where(
        i < half, n_h // 2 - half * (ck + 1) + i, n_h // 2 + half * ck + i - half
    )
    expert = ((h + delta) % n_h) * 2 + expert_local
    named = jnp.zeros((toks, total), F32)
    gates = jnp.zeros((toks, total), F32)
    for k in range(top):
        hit = (ids_ref[:, k : k + 1] == expert).astype(F32)
        named = named + hit
        gates = gates + hit * gw_ref[:, k : k + 1]
    earlier = (iota((toks, toks), 1) < iota((toks, toks), 0)).astype(BF)
    rank = dot(earlier, named.astype(BF))
    taken = named * (rank == place.astype(F32)).astype(F32)
    gates = gates * taken
    hi = gates.astype(BF)
    rest = gates - hi.astype(F32)
    mid = rest.astype(BF)
    lo = (rest - mid.astype(F32)).astype(BF)
    pick = taken.astype(BF)
    pieces = []
    for value, w in ((pick, 0), (hi, 1), (mid, 1), (lo, 1)):
        for p in range(2):
            pieces.append(value * ((which == w) & (part == p)).astype(BF))
    sel[...] = jnp.concatenate(pieces, axis=0)

    size = depth * 16

    def row_order(q):
        p, w = q // (size // 2), (q // (size // 4)) % 2
        e, t, c = (q // rows) % 2, (q // CAP) % depth, q % CAP
        return t * 16 + w * 8 + p * 4 + e * 2 + c

    unperm[...] = (row_order(iota((size, size), 0)) == iota((size, size), 1)).astype(BF)
    perm[...] = (row_order(iota((size, size), 1)) == iota((size, size), 0)).astype(BF)

    loads[0].wait()
    loads[1].wait()
    t0, t1 = tok[:, :LANES], tok[:, LANES:]
    g0, g1 = grd[:, :LANES], grd[:, LANES:]
    rhs = jnp.concatenate([t0, t1, g0, g1, g0, g1, g0, g1], axis=0)
    tile_s[...] = dot(sel[...], rhs, TN).astype(BF).reshape(n_h, 16, LANES)
    home = (chunks - 1) * depth
    tile_r[home] = tile_s[home]

    pl.semaphore_wait(barrier, n_h - 1 + n_j - 1 + n_g - 1)

    def distance(c, t):
        return jnp.where(
            t < half, n_h // 2 - half * (c + 1) + t, n_h // 2 + half * c + t - half
        )

    def z_send(c, src, dst, sign, send, recv):
        def body(t, carry):
            at = c * depth + t
            peer = lax.rem(h + n_h + sign * distance(c, t), n_h)
            pltpu.make_async_remote_copy(
                src.at[at], dst.at[at], send, recv, (g, j, peer), MESH
            ).start()
            return carry

        lax.fori_loop(1 if c == chunks - 1 else 0, depth, body, 0)

    def z_block(c, ref):
        return ref.at[pl.ds(c * depth + (c == chunks - 1), depth - (c == chunks - 1))]

    def wait_recv(ref, sem):
        pltpu.make_async_remote_copy(ref, ref, sem, sem, in_peer(1), MESH).wait_recv()

    def wait_send(ref, sem):
        pltpu.make_async_remote_copy(ref, ref, sem, sem, in_peer(1), MESH).wait_send()

    for c in range(chunks):
        z_send(c, tile_s, tile_r, 1, send_sem.at[0], z_sem.at[c])

    for c in range(chunks):
        wait_recv(z_block(c, tile_r), z_sem.at[c])
        tiles = tile_r[c * depth : (c + 1) * depth].reshape(size, LANES)
        ordered = dot(unperm[...], tiles).astype(BF)
        acts[j, c, :, :, :, :LANES] = ordered[: size // 2].reshape(2, 2, rows, LANES)
        acts[j, c, :, :, :, LANES:] = ordered[size // 2 :].reshape(2, 2, rows, LANES)

        def forward(o, carry, c=c):
            pltpu.make_async_remote_copy(
                acts.at[j, c], acts.at[j, c], send_sem.at[1], y_sem, in_peer(o), MESH
            ).start()
            return carry

        lax.fori_loop(1, n_j, forward, 0)
    for load in loads[2:]:
        load.wait()
    wait_recv(acts.at[pl.ds(0, n_j - 1)], y_sem)

    wide = n_j // n_g

    def rows_out(o, carry):
        there = lax.rem(g + o, n_g)
        pltpu.make_async_remote_copy(
            acts.at[pl.ds(there * wide, wide)], xg_r.at[g],
            send_sem.at[2], xg_sem, (there, j, h), MESH,
        ).start()
        return carry

    m = chunks * rows
    units = wg.shape[2]
    for e in range(2):
        gate_pre = jnp.zeros((m, units), F32)
        up_pre = jnp.zeros((m, units), F32)
        d_hidden = jnp.zeros((m, units), F32)
        for b in range(n_j):
            cols = slice(b * width, (b + 1) * width)
            x = acts[b, :, 0, e].reshape(m, width)
            gated = acts[b, :, 1, e].reshape(m, width)
            gate_pre = gate_pre + dot(x, wg[e, cols, :])
            up_pre = up_pre + dot(x, wu[e, cols, :])
            d_hidden = d_hidden + dot(gated, wd[e, :, cols], NT)
        sig = jax.nn.sigmoid(gate_pre)
        silu = gate_pre * sig
        hr[g, 0, e] = (silu * up_pre).astype(BF)
        d_gate = d_hidden * up_pre * sig * (1.0 + gate_pre * (1.0 - sig))
        hr[g, 1, e] = d_gate.astype(BF)
        hr[g, 2, e] = (d_hidden * silu).astype(BF)

    def hidden_out(o, carry):
        pltpu.make_async_remote_copy(
            hr.at[g], hr.at[g], send_sem.at[3], hr_sem, group_peer(o), MESH
        ).start()
        return carry

    def part_out(o, c):
        return pltpu.make_async_remote_copy(
            part_s.at[lax.rem(j + o, n_j), c], part_r.at[o - 1, c],
            send_sem.at[4], rs_sem.at[c], in_peer(o), MESH,
        )

    for e in range(2):
        hidden, d_gate, d_up = hr[g, 0, e], hr[g, 1, e], hr[g, 2, e]
        for b in range(n_j):
            cols = slice(b * width, (b + 1) * width)
            out = dot(hidden, wd[e, :, cols]).astype(BF)
            part_s[b, :, 1, e] = out.reshape(chunks, rows, width)
            back = dot(d_gate, wg[e, cols, :], NT) + dot(d_up, wu[e, cols, :], NT)
            part_s[b, :, 0, e] = back.astype(BF).reshape(chunks, rows, width)

    for c in range(chunks):

        def send_part(o, carry, c=c):
            part_out(o, c).start()
            return carry

        lax.fori_loop(1, n_j, send_part, 0)
    lax.fori_loop(1, n_g, hidden_out, 0)
    lax.fori_loop(1, n_g, rows_out, 0)

    for c in range(chunks):
        wait_recv(part_r.at[:, c], rs_sem.at[c])
        summed = part_s[j, c].astype(F32)
        for o in range(n_j - 1):
            summed = summed + part_r[o, c].astype(F32)
        summed = summed.astype(BF)
        both = jnp.concatenate(
            [
                summed[..., :LANES].reshape(size // 2, LANES),
                summed[..., LANES:].reshape(size // 2, LANES),
            ],
            axis=0,
        )
        tiles = dot(perm[...], both).astype(BF)
        back_s[c * depth : (c + 1) * depth] = tiles.reshape(depth, 16, LANES)
        z_send(c, back_s, back_r, -1, send_sem.at[5], zb_sem)
    back_r[home] = back_s[home]

    wait_recv(hr.at[pl.ds(0, n_g - 1)], hr_sem)
    wait_recv(xg_r.at[pl.ds(0, n_g - 1)], xg_sem)
    xg_r[g] = acts[pl.ds(g * wide, wide)]
    for e in range(2):
        ups = [hr[:, n, e].reshape(n_g * m, units) for n in range(3)]
        for b in range(wide):
            cols = slice(b * width, (b + 1) * width)
            x = xg_r[:, b, :, 0, e].reshape(n_g * m, width)
            gated = xg_r[:, b, :, 1, e].reshape(n_g * m, width)
            og[e, cols, :] = dot(x, ups[1], TN)
            ou[e, cols, :] = dot(x, ups[2], TN)
            od[e, :, cols] = dot(ups[0], gated, TN)
    stores = [
        pltpu.make_async_copy(src, dst, out_sem.at[n])
        for n, (src, dst) in enumerate(((og, gg_hbm), (ou, gu_hbm), (od, gd_hbm)))
    ]
    for store in stores:
        store.start()

    wait_recv(back_r.at[pl.ds(0, n_h - 1)], zb_sem)
    sums = dot(sel[...], back_r[...].reshape(total, LANES))
    at = [sums[n * toks : (n + 1) * toks] for n in range(8)]
    gtok_ref[:, :LANES] = at[0].astype(BF)
    gtok_ref[:, LANES:] = at[1].astype(BF)
    mixed_ref[:, :LANES] = (at[2] + at[4] + at[6]).astype(BF)
    mixed_ref[:, LANES:] = (at[3] + at[5] + at[7]).astype(BF)

    wait_send(tile_s.at[pl.ds(0, n_h - 1)], send_sem.at[0])
    wait_send(acts.at[pl.ds(0, n_j - 1)], send_sem.at[1])
    wait_send(xg_r.at[pl.ds(0, n_g - 1)], send_sem.at[2])
    wait_send(hr.at[pl.ds(0, n_g - 1)], send_sem.at[3])
    wait_send(part_r, send_sem.at[4])
    wait_send(back_s.at[pl.ds(0, n_h - 1)], send_sem.at[5])
    for store in stores:
        store.wait()


def layer(tokens, grad_mixed, expert_ids, gate_weight, w_gate, w_up, w_down):
    n_g, n_j, n_h = (lax.axis_size(a) for a in ("group", "ingroup", "hid"))
    per, d_model, units = w_gate.shape
    toks, top = expert_ids.shape
    depth = min(8, n_h // 2)
    chunks = n_h // depth
    rows = depth * CAP
    width = 2 * LANES
    wide = n_j // n_g
    m = chunks * rows
    share = d_model // n_g
    vmem, hbm = pl.BlockSpec(memory_space=pltpu.VMEM), pl.BlockSpec(memory_space=pl.ANY)
    block = (chunks, 2, per, rows, width)
    dma = pltpu.SemaphoreType.DMA
    return pl.pallas_call(
        functools.partial(kernel, (n_g, n_j, n_h, chunks, depth, per, top)),
        out_shape=(
            jax.ShapeDtypeStruct((toks, width), BF),
            jax.ShapeDtypeStruct((toks, width), BF),
            jax.ShapeDtypeStruct((per, share, units), F32),
            jax.ShapeDtypeStruct((per, share, units), F32),
            jax.ShapeDtypeStruct((per, units, share), F32),
        ),
        in_specs=[vmem] * 2 + [hbm] * 5,
        out_specs=(vmem, vmem, hbm, hbm, hbm),
        scratch_shapes=[
            pltpu.VMEM((toks, width), BF),
            pltpu.VMEM((toks, width), BF),
            pltpu.VMEM(w_gate.shape, BF),
            pltpu.VMEM(w_up.shape, BF),
            pltpu.VMEM(w_down.shape, BF),
            pltpu.VMEM((8 * toks, n_h * 16), BF),
            pltpu.VMEM((depth * 16, depth * 16), BF),
            pltpu.VMEM((depth * 16, depth * 16), BF),
            pltpu.VMEM((n_h, 16, LANES), BF),
            pltpu.VMEM((n_h, 16, LANES), BF),
            pltpu.VMEM((n_j, *block), BF),
            pltpu.VMEM((n_j, *block), BF),
            pltpu.VMEM((n_j - 1, *block), BF),
            pltpu.VMEM((n_h, 16, LANES), BF),
            pltpu.VMEM((n_h, 16, LANES), BF),
            pltpu.VMEM((n_g, wide, *block), BF),
            pltpu.VMEM((n_g, 3, per, m, units), BF),
            pltpu.VMEM((per, share, units), F32),
            pltpu.VMEM((per, share, units), F32),
            pltpu.VMEM((per, units, share), F32),
            dma((5,)),
            dma((3,)),
            dma((6,)),
            dma((chunks,)),
            dma,
            dma((chunks,)),
            dma,
            dma,
            dma,
        ],
        compiler_params=pltpu.CompilerParams(
            collective_id=0, has_side_effects=True, vmem_limit_bytes=48 * 2**20
        ),
    )(expert_ids, gate_weight, tokens, grad_mixed, w_gate, w_up, w_down)


def solution(mesh):
    both = P(("group", "hid"), None)
    return jax.shard_map(
        layer,
        mesh=mesh,
        in_specs=(
            both,
            both,
            both,
            both,
            P("hid", None, "ingroup"),
            P("hid", None, "ingroup"),
            P("hid", "ingroup", None),
        ),
        out_specs=(
            P(("group", "hid"), "ingroup"),
            P(("group", "hid"), "ingroup"),
            P("hid", "group", "ingroup"),
            P("hid", "group", "ingroup"),
            P("hid", "ingroup", "group"),
        ),
        check_vma=False,
    )
```

time: 225 us -> 98.4 us (0.44)
  Pallas kernels: 0 us -> 80.8 us
  blocking collectives: 77.9 us -> 0 us
  waiting for transfers between devices: 71.6 us -> 0 us
  starting transfers between devices: 22.8 us -> 0 us
  between operations: 14.1 us -> 0.66 us
  other arithmetic: 8.51 us -> 0 us
  matrix products: 7.14 us -> 0 us
  local copies, waits for them, and re-layouts: 22.4 us -> 15.9 us
    pallas_call x0 -> x1, Pallas kernels: none -> 80.8 us  [layer(): pl.pallas_call(functools.partial(kernel, (n_g, n_j, n_h, chunks, depth, p...]
    all_to_all x2 -> x0, blocking collectives: 77.9 us -> none  [the longest x1 58.8 us: sent_together(): lax.all_to_all(both, axis, split_axis=split_dim, concat_axis=concat_dim,...]
    all_to_all x1 -> x0, waiting for transfers between devices: 29.3 us -> none  [sent_together(): lax.all_to_all(both, axis, split_axis=split_dim, concat_axis=concat_dim,...]
    all_gather x1 -> x0, waiting for transfers between devices: 25.1 us -> none  [sent_together_2(): result = lax.all_gather(both, axis, axis=dim, tiled=True)]
    all_to_all x1 -> x0, starting transfers between devices: 22.6 us -> none  [sent_together(): lax.all_to_all(both, axis, split_axis=split_dim, concat_axis=concat_dim,...]
    reduce_scatter x2 -> x0, waiting for transfers between devices: 17.2 us -> none  [the longest x1 17.2 us: side_by_side(): lax.psum_scatter(both, axis, scatter_dimension=dim, tiled=True)]
    unnamed x14 -> x27, local copies, waits for them, and re-layouts: 3.97 us -> 13.5 us
    dot_general x9 -> x0, matrix products: 7.14 us -> none  [the longest x1 1.75 us: shards(): jnp.einsum('emh,ehd->emd', hidden, w_down, preferred_element_type=jnp.flo...]
  transfers between devices with their start and end apart: 4 -> 0, of which waited for: 3 -> 0; matrix products, arithmetic and copies ran while one was open for 5% -> 0% of each run, Pallas kernels for 0% -> 0%
where the time goes in v1:
time: 98.4 us; the launch traced here: 97.4 us
  Pallas kernels  80.8 us (82%)
  local copies, waits for them, and re-layouts  15.9 us (16%)
    pallas_call x1, Pallas kernels, layer(): pl.pallas_call(functools.partial(kernel, (n_g, n_j, n_h, chunks, depth, p...  80.8 us
    unnamed x27, local copies, waits for them, and re-layouts  13.5 us
    pallas_call x2, local copies, waits for them, and re-layouts, layer(): pl.pallas_call(functools.partial(kernel, (n_g, n_j, n_h, chunks, depth, p...  2.34 us

profile of v1, /device:TPU:1, one launch (start us, length us, event | category | flops | bytes accessed | tf_op | source)
XLA Modules:
  0.0 97.4 jit_solution(15400365383870087201)
XLA Ops:
  0.6 0.8 copy.12.ids_ref
  1.4 0.8 copy.13.gw_ref
  2.2 0.0 copy-start.9
  2.2 3.8 %copy.14.wg_hbm = bf16[2,2048,176]{2,1,0:T(8,128)(2,1)} copy(bf16[2,2048,176]{1,2,0:T(8,128)(2,1)} %param.11) | data formatting | bytes 2883584 | tf_op args[4]
  5.9 0.0 copy-done.9
  5.9 0.0 copy-start
  5.9 2.4 %copy.15.wu_hbm = bf16[2,2048,176]{2,1,0:T(8,128)(2,1)} copy(bf16[2,2048,176]{1,2,0:T(8,128)(2,1)S(1)} %copy-done.9) | data formatting | bytes 2883584 | tf_op args[5]
  8.4 0.0 copy-done
  8.4 0.0 copy-start.3
  8.4 0.8 copy-done.3
  9.2 0.0 copy-start.4
  9.2 0.8 copy-done.4
  10.1 80.8 %shard_map.110 = (bf16[16,256]{1,0:T(8,128)(2,1)S(1)}, bf16[16,256]{1,0:T(8,128)(2,1)S(1)}, f32[2,512,176]{2,1,0:T(8,128)S(1)}, f32[2,512,176]{2,1,0:T(8,128)S(1)}, f32[2,176,512]{2,1,0:T(8,128)S(1)}) custom-call(s32[16,6]{1,0:T(8,128)S(1)} %copy.12.ids_ref, f32[16,6]{1,0:T(8,128)S(1)} %copy.13.gw_ref, bf16[16,2048]{1,0:T(8,128)(2,1)S(1)} %copy-done.3, ...), custom_call_target="tpu_custom_call" | custom-call | tf_op jit(solution)/shard_map/pallas_call | solution.py:313
  90.9 0.0 copy-start.1
  90.9 0.8 copy-done.1
  91.8 0.0 copy-start.5
  91.8 0.6 copy-done.5
  92.3 0.0 copy-start.7
  92.4 0.6 copy-done.7
  92.9 0.0 copy-start.8
  92.9 0.0 copy-start.6
  93.0 0.0 copy-start.2
  93.0 1.2 %copy.16 = f32[2,512,176]{1,2,0:T(8,128)} copy(f32[2,512,176]{2,1,0:T(8,128)S(1)} %get-tuple-element.7) | data formatting | bytes 1441792 | tf_op jit(solution)/shard_map/pallas_call | solution.py:313
  94.1 1.2 %copy.17 = f32[2,512,176]{1,2,0:T(8,128)} copy(f32[2,512,176]{2,1,0:T(8,128)S(1)} %get-tuple-element.8) | data formatting | bytes 1441792 | tf_op jit(solution)/shard_map/pallas_call | solution.py:313
  95.3 0.0 copy-done.8
  95.3 0.6 copy.21
  95.9 0.0 copy-done.6
  95.9 0.6 copy.22
  96.5 0.0 copy-done.2
  96.5 0.9 copy.23
Async XLA Ops:
  2.2 3.8 %copy-start.9 = (bf16[2,2048,176]{1,2,0:T(8,128)(2,1)S(1)}, bf16[2,2048,176]{1,2,0:T(8,128)(2,1)}, u32[]{:S(2)}) copy-start(bf16[2,2048,176]{1,2,0:T(8,128)(2,1)} %param.12) | copy-start | bytes 4325380
  5.9 2.4 %copy-start = (bf16[2,176,2048]{2,1,0:T(8,128)(2,1)S(1)}, bf16[2,176,2048]{2,1,0:T(8,128)(2,1)}, u32[]{:S(2)}) copy-start(bf16[2,176,2048]{2,1,0:T(8,128)(2,1)} %wd_hbm.1) | copy-start | bytes 4325380
  8.4 0.8 copy-start.3
  9.2 0.8 copy-start.4
  90.9 0.9 copy-start.1
  91.8 0.6 copy-start.5
  92.3 0.6 copy-start.7
  92.9 2.4 %copy-start.8 = (bf16[16,256]{1,0:T(8,128)(2,1)S(1)}, bf16[16,256]{1,0:T(8,128)(2,1)}, u32[]{:S(2)}) copy-start(bf16[16,256]{1,0:T(8,128)(2,1)} %copy-done.7) | copy-start | bytes 24580
  92.9 3.0 %copy-start.6 = (bf16[16,256]{1,0:T(8,128)(2,1)S(1)}, bf16[16,256]{1,0:T(8,128)(2,1)}, u32[]{:S(2)}) copy-start(bf16[16,256]{1,0:T(8,128)(2,1)} %copy-done.5) | copy-start | bytes 24580
  93.0 3.6 %copy-start.2 = (f32[2,176,512]{2,1,0:T(8,128)S(1)}, f32[2,176,512]{2,1,0:T(8,128)}, u32[]{:S(2)}) copy-start(f32[2,176,512]{2,1,0:T(8,128)} %copy-done.1) | copy-start | bytes 2162692

commit v2 on v1

v2 whole, which is shorter than its diff:
```python
import functools

import jax
import jax.numpy as jnp
from jax import lax
from jax.experimental import pallas as pl
from jax.experimental.pallas import tpu as pltpu
from jax.sharding import PartitionSpec as P

MESH = pl.DeviceIdType.MESH
BF = jnp.bfloat16
F32 = jnp.float32
CAP = 2
LANES = 128

NN = (((1,), (0,)), ((), ()))
NT = (((1,), (1,)), ((), ()))
TN = (((0,), (0,)), ((), ()))


def dot(a, b, dims=NN):
    return lax.dot_general(a, b, dims, preferred_element_type=F32)


def iota(shape, dim):
    return lax.broadcasted_iota(jnp.int32, shape, dim)


def kernel(
    dims,
    ids_hbm, gw_hbm, tok_hbm, grd_hbm, wg_hbm, wu_hbm, wd_hbm,
    mixed_hbm, gtok_hbm, gg_hbm, gu_hbm, gd_hbm,
    ids, gw, tok, grd, wg, wu, wd, sel, unperm, perm,
    tile_s, tile_r, acts, part_s, twin_r, pair_s, part_r, back_s, back_r,
    xg_r, hr, mixed, gtok, og, ou, od,
    in_sem, out_sem, send_sem, z_sem, y_sem, twin_sem, pair_sem, rs_sem, zb_sem, xg_sem, hr_sem,
):
    n_g, n_j, n_h, chunks, depth, per, top = dims
    rows = depth * CAP
    half = depth // 2
    toks = ids_hbm.shape[1]
    g, j, h = lax.axis_index("group"), lax.axis_index("ingroup"), lax.axis_index("hid")
    width = 2 * LANES

    lanes = pl.ds(pl.multiple_of(j * width, width), width)
    loads = [
        pltpu.make_async_copy(src, dst, in_sem.at[n])
        for n, (src, dst) in enumerate(
            (
                (ids_hbm, ids),
                (gw_hbm, gw),
                (tok_hbm.at[:, lanes], tok),
                (grd_hbm.at[:, lanes], grd),
                (wg_hbm, wg),
                (wu_hbm, wu),
                (wd_hbm, wd),
            )
        )
    ]
    for load in loads:
        load.start()
    sent = []

    barrier = pltpu.get_barrier_semaphore()

    def greet(count, device):
        def body(o, carry):
            pl.semaphore_signal(
                barrier, inc=1, device_id=device(o), device_id_type=MESH
            )
            return carry

        lax.fori_loop(1, count, body, 0)

    def hid_peer(o):
        return (g, j, lax.rem(h + o, n_h))

    n_y, y, core = n_j // 2, j // 2, j % 2
    twin = (g, 2 * y + 1 - core, h)

    def y_at(o):
        return lax.rem(y + o, n_y)

    def y_peer(o):
        return (g, 2 * y_at(o) + core, h)

    def group_peer(o):
        return (lax.rem(g + o, n_g), j, h)

    greet(n_h, hid_peer)
    greet(n_y, y_peer)
    pl.semaphore_signal(barrier, inc=1, device_id=twin, device_id_type=MESH)
    greet(n_g, group_peer)

    total = n_h * 16
    lane = iota((1, total), 1)
    pos = lane // 16
    which, part = (lane // 8) % 2, (lane // 4) % 2
    expert_local, place = (lane // 2) % 2, lane % 2
    ck, i = pos // depth, pos % depth
    delta = jnp.where(
        i < half, n_h // 2 - half * (ck + 1) + i, n_h // 2 + half * ck + i - half
    )
    expert = ((h + delta) % n_h) * 2 + expert_local
    named = jnp.zeros((toks, total), F32)
    gates = jnp.zeros((toks, total), F32)
    loads[0].wait()
    loads[1].wait()
    same = iota((toks, toks), 0) == iota((toks, toks), 1)

    def column(row):
        return jnp.sum(jnp.where(same, row.astype(F32), 0.0), axis=1, keepdims=True)

    wanted = expert.astype(F32)
    for k in range(top):
        hit = (column(ids[k : k + 1, :]) == wanted).astype(F32)
        named = named + hit
        gates = gates + hit * column(gw[k : k + 1, :])
    earlier = (iota((toks, toks), 1) < iota((toks, toks), 0)).astype(BF)
    rank = dot(earlier, named.astype(BF))
    taken = named * (rank == place.astype(F32)).astype(F32)
    gates = gates * taken
    hi = gates.astype(BF)
    rest = gates - hi.astype(F32)
    mid = rest.astype(BF)
    lo = (rest - mid.astype(F32)).astype(BF)
    pick = taken.astype(BF)
    pieces = []
    for value, w in ((pick, 0), (hi, 1), (mid, 1), (lo, 1)):
        for p in range(2):
            pieces.append(value * ((which == w) & (part == p)).astype(BF))
    sel[...] = jnp.concatenate(pieces, axis=0)

    size = depth * 16

    def row_order(q):
        p, w = q // (size // 2), (q // (size // 4)) % 2
        e, t, c = (q // rows) % 2, (q // CAP) % depth, q % CAP
        return t * 16 + w * 8 + p * 4 + e * 2 + c

    unperm[...] = (row_order(iota((size, size), 0)) == iota((size, size), 1)).astype(BF)
    perm[...] = (row_order(iota((size, size), 1)) == iota((size, size), 0)).astype(BF)

    loads[2].wait()
    loads[3].wait()
    t0, t1 = tok[:, :LANES], tok[:, LANES:]
    g0, g1 = grd[:, :LANES], grd[:, LANES:]
    rhs = jnp.concatenate([t0, t1, g0, g1, g0, g1, g0, g1], axis=0)
    tile_s[...] = dot(sel[...], rhs, TN).astype(BF).reshape(n_h, 16, LANES)
    home = (chunks - 1) * depth
    tile_r[home] = tile_s[home]

    pl.semaphore_wait(barrier, n_h - 1 + n_y - 1 + 1 + n_g - 1)

    def wait_recv(ref, sem):
        pltpu.make_async_remote_copy(ref, ref, sem, sem, twin, MESH).wait_recv()

    def wait_send(ref, sem):
        pltpu.make_async_remote_copy(ref, ref, sem, sem, twin, MESH).wait_send()

    def distance(c, t):
        return jnp.where(
            t < half, n_h // 2 - half * (c + 1) + t, n_h // 2 + half * c + t - half
        )

    def z_send(c, src, dst, sign, send, recv):
        def body(t, carry):
            t = jnp.where(t % 2 == 0, t // 2, depth - 1 - t // 2)
            at = c * depth + t
            peer = lax.rem(h + n_h + sign * distance(c, t), n_h)
            pltpu.make_async_remote_copy(
                src.at[at], dst.at[at], send, recv, (g, j, peer), MESH
            ).start()
            return carry

        lax.fori_loop(1 if c == chunks - 1 else 0, depth, body, 0)

    def z_block(c, ref):
        return ref.at[pl.ds(c * depth + (c == chunks - 1), depth - (c == chunks - 1))]

    last = chunks - 1
    order = [*range(last - 1), last, last - 1]
    for c in order:
        z_send(c, tile_s, tile_r, 1, send_sem.at[0], z_sem.at[c])
    sent.append((tile_s.at[pl.ds(0, n_h - 1)], send_sem.at[0]))

    def to_twin(b, c):
        pltpu.make_async_remote_copy(
            acts.at[b, c], acts.at[b, c], send_sem.at[6], twin_sem, twin, MESH
        ).start()

    def pass_on(c):
        wait_recv(acts.at[pl.ds(0, n_y - 1), c], y_sem.at[c])

        def body(o, carry):
            to_twin(2 * y_at(o) + core, c)
            return carry

        lax.fori_loop(1, n_y, body, 0)

    before = None
    for c in (last, *range(last)):
        wait_recv(z_block(c, tile_r), z_sem.at[c])
        tiles = tile_r[c * depth : (c + 1) * depth].reshape(size, LANES)
        ordered = dot(unperm[...], tiles).astype(BF)
        acts[j, c, :, :, :, :LANES] = ordered[: size // 2].reshape(2, 2, rows, LANES)
        acts[j, c, :, :, :, LANES:] = ordered[size // 2 :].reshape(2, 2, rows, LANES)

        def forward(o, carry, c=c):
            pltpu.make_async_remote_copy(
                acts.at[j, c], acts.at[j, c],
                send_sem.at[1], y_sem.at[c], y_peer(o), MESH,
            ).start()
            return carry

        lax.fori_loop(1, n_y, forward, 0)
        to_twin(j, c)
        if before is not None:
            pass_on(before)
        before = c
    pass_on(before)
    sent.append((acts.at[pl.ds(0, n_y - 1)], send_sem.at[1]))
    sent.append((acts.at[pl.ds(0, n_y)], send_sem.at[6]))
    for load in loads[4:]:
        load.wait()
    wait_recv(acts.at[pl.ds(0, n_y)], twin_sem)

    wide = n_j // n_g

    def rows_out(o, carry):
        there = lax.rem(g + o, n_g)
        pltpu.make_async_remote_copy(
            acts.at[pl.ds(there * wide, wide)], xg_r.at[g],
            send_sem.at[2], xg_sem, (there, j, h), MESH,
        ).start()
        return carry

    lax.fori_loop(1, n_g, rows_out, 0)
    sent.append((xg_r.at[pl.ds(0, n_g - 1)], send_sem.at[2]))

    m = chunks * rows
    units = wg.shape[1]
    hiddens = []
    for e in range(2):
        gate_pre = jnp.zeros((m, units), F32)
        up_pre = jnp.zeros((m, units), F32)
        d_hidden = jnp.zeros((m, units), F32)
        for b in range(n_j):
            cols = slice(b * width, (b + 1) * width)
            x = acts[b, :, 0, e].reshape(m, width)
            gated = acts[b, :, 1, e].reshape(m, width)
            gate_pre = gate_pre + dot(x, wg[e, :, cols], NT)
            up_pre = up_pre + dot(x, wu[e, :, cols], NT)
            d_hidden = d_hidden + dot(gated, wd[e, :, cols], NT)
        sig = jax.nn.sigmoid(gate_pre)
        silu = gate_pre * sig
        d_gate = d_hidden * up_pre * sig * (1.0 + gate_pre * (1.0 - sig))
        hiddens.append(
            [v.astype(BF) for v in (silu * up_pre, d_gate, d_hidden * silu)]
        )
    for n in range(3):
        hr[g, n] = jnp.concatenate([hiddens[0][n], hiddens[1][n]], axis=1)

    def hidden_out(o, carry):
        pltpu.make_async_remote_copy(
            hr.at[g], hr.at[g], send_sem.at[3], hr_sem, group_peer(o), MESH
        ).start()
        return carry

    lax.fori_loop(1, n_g, hidden_out, 0)
    sent.append((hr.at[pl.ds(0, n_g - 1)], send_sem.at[3]))

    for e in range(2):
        hidden, d_gate, d_up = hiddens[e]
        for b in range(n_j):
            cols = slice(b * width, (b + 1) * width)
            out = dot(hidden, wd[e, :, cols]).astype(BF)
            part_s[b, :, 1, e] = out.reshape(chunks, rows, width)
            back = dot(d_gate, wg[e, :, cols]) + dot(d_up, wu[e, :, cols])
            part_s[b, :, 0, e] = back.astype(BF).reshape(chunks, rows, width)

    for c in range(chunks):

        def twin_part(b, carry, c=c):
            pltpu.make_async_remote_copy(
                part_s.at[2 * b + 1 - core, c], twin_r.at[b, c],
                send_sem.at[7], pair_sem.at[c], twin, MESH,
            ).start()
            return carry

        lax.fori_loop(0, n_y, twin_part, 0)
    sent.append((twin_r, send_sem.at[7]))

    def pair(c):
        wait_recv(twin_r.at[:, c], pair_sem.at[c])

        def body(o, carry):
            there = y_at(o)
            mine = part_s[2 * there + core, c].astype(F32)
            pair_s[there, c] = (mine + twin_r[there, c].astype(F32)).astype(BF)
            pltpu.make_async_remote_copy(
                pair_s.at[there, c], part_r.at[o - 1, c],
                send_sem.at[4], rs_sem.at[c], y_peer(o), MESH,
            ).start()
            return carry

        lax.fori_loop(1, n_y, body, 0)

    for c in range(chunks):
        if c == 0:
            pair(0)
        if c + 1 < chunks:
            pair(c + 1)
        summed = part_s[j, c].astype(F32) + twin_r[y, c].astype(F32)
        wait_recv(part_r.at[:, c], rs_sem.at[c])
        for o in range(n_y - 1):
            summed = summed + part_r[o, c].astype(F32)
        summed = summed.astype(BF)
        both = jnp.concatenate(
            [
                summed[..., :LANES].reshape(size // 2, LANES),
                summed[..., LANES:].reshape(size // 2, LANES),
            ],
            axis=0,
        )
        tiles = dot(perm[...], both).astype(BF)
        back_s[c * depth : (c + 1) * depth] = tiles.reshape(depth, 16, LANES)
        z_send(c, back_s, back_r, -1, send_sem.at[5], zb_sem)
    sent.append((part_r, send_sem.at[4]))
    sent.append((back_s.at[pl.ds(0, n_h - 1)], send_sem.at[5]))
    back_r[home] = back_s[home]

    wait_recv(hr.at[pl.ds(0, n_g - 1)], hr_sem)
    wait_recv(xg_r.at[pl.ds(0, n_g - 1)], xg_sem)
    xg_r[g] = acts[pl.ds(g * wide, wide)]
    for e in range(2):
        mine = slice(e * units, (e + 1) * units)
        ups = [hr[:, n, :, mine].reshape(n_g * m, units) for n in range(3)]
        for b in range(wide):
            cols = slice(b * width, (b + 1) * width)
            x = xg_r[:, b, :, 0, e].reshape(n_g * m, width)
            gated = xg_r[:, b, :, 1, e].reshape(n_g * m, width)
            og[e, :, cols] = dot(ups[1], x, TN)
            ou[e, :, cols] = dot(ups[2], x, TN)
            od[e, :, cols] = dot(ups[0], gated, TN)
    stores = [
        pltpu.make_async_copy(src, dst, out_sem.at[n])
        for n, (src, dst) in enumerate(
            (
                (og, gg_hbm),
                (ou, gu_hbm),
                (od, gd_hbm),
                (mixed, mixed_hbm),
                (gtok, gtok_hbm),
            )
        )
    ]
    for store in stores[:3]:
        store.start()

    wait_recv(back_r.at[pl.ds(0, n_h - 1)], zb_sem)
    sums = dot(sel[...], back_r[...].reshape(total, LANES))
    at = [sums[n * toks : (n + 1) * toks] for n in range(8)]
    gtok[:, :LANES] = at[0].astype(BF)
    gtok[:, LANES:] = at[1].astype(BF)
    mixed[:, :LANES] = (at[2] + at[4] + at[6]).astype(BF)
    mixed[:, LANES:] = (at[3] + at[5] + at[7]).astype(BF)

    for store in stores[3:]:
        store.start()

    for ref, sem in sent:
        wait_send(ref, sem)
    for store in stores:
        store.wait()


def hand_over(a, b, c, d, e, ao, bo, co, do, eo, av, bv, cv, dv, ev, get_sem, put_sem):
    gets, puts = [], []
    for n, (src, held, dst) in enumerate(
        ((a, av, ao), (b, bv, bo), (c, cv, co), (d, dv, do), (e, ev, eo))
    ):
        gets.append(pltpu.make_async_copy(src, held, get_sem.at[n]))
        puts.append(pltpu.make_async_copy(held, dst, put_sem.at[n]))
    for get in gets:
        get.start()
    for get, put in zip(gets, puts, strict=True):
        get.wait()
        put.start()
    for put in puts:
        put.wait()


def layer(tokens, grad_mixed, expert_ids, gate_weight, w_gate, w_up, w_down):
    expert_ids, gate_weight = expert_ids.T, gate_weight.T
    w_gate, w_up = jnp.swapaxes(w_gate, 1, 2), jnp.swapaxes(w_up, 1, 2)
    n_g, n_j, n_h = (lax.axis_size(a) for a in ("group", "ingroup", "hid"))
    per, units, d_model = w_gate.shape
    top, toks = expert_ids.shape
    depth = min(8, n_h // 2)
    chunks = n_h // depth
    rows = depth * CAP
    width = 2 * LANES
    wide = n_j // n_g
    m = chunks * rows
    share = d_model // n_g
    hbm = pl.BlockSpec(memory_space=pl.ANY)
    block = (chunks, 2, per, rows, width)
    dma = pltpu.SemaphoreType.DMA
    outs = pl.pallas_call(
        functools.partial(kernel, (n_g, n_j, n_h, chunks, depth, per, top)),
        out_shape=(
            jax.ShapeDtypeStruct((toks, width), BF),
            jax.ShapeDtypeStruct((toks, width), BF),
            jax.ShapeDtypeStruct((per, units, share), F32),
            jax.ShapeDtypeStruct((per, units, share), F32),
            jax.ShapeDtypeStruct((per, units, share), F32),
        ),
        in_specs=[hbm] * 7,
        out_specs=(hbm,) * 5,
        scratch_shapes=[
            pltpu.VMEM((top, toks), jnp.int32),
            pltpu.VMEM((top, toks), F32),
            pltpu.VMEM((toks, width), BF),
            pltpu.VMEM((toks, width), BF),
            pltpu.VMEM(w_gate.shape, BF),
            pltpu.VMEM(w_up.shape, BF),
            pltpu.VMEM(w_down.shape, BF),
            pltpu.VMEM((8 * toks, n_h * 16), BF),
            pltpu.VMEM((depth * 16, depth * 16), BF),
            pltpu.VMEM((depth * 16, depth * 16), BF),
            pltpu.VMEM((n_h, 16, LANES), BF),
            pltpu.VMEM((n_h, 16, LANES), BF),
            pltpu.VMEM((n_j, *block), BF),
            pltpu.VMEM((n_j, *block), BF),
            pltpu.VMEM((n_j // 2, *block), BF),
            pltpu.VMEM((n_j // 2, *block), BF),
            pltpu.VMEM((n_j // 2 - 1, *block), BF),
            pltpu.VMEM((n_h, 16, LANES), BF),
            pltpu.VMEM((n_h, 16, LANES), BF),
            pltpu.VMEM((n_g, wide, *block), BF),
            pltpu.VMEM((n_g, 3, m, per * units), BF),
            pltpu.VMEM((toks, width), BF),
            pltpu.VMEM((toks, width), BF),
            pltpu.VMEM((per, units, share), F32),
            pltpu.VMEM((per, units, share), F32),
            pltpu.VMEM((per, units, share), F32),
            dma((7,)),
            dma((5,)),
            dma((8,)),
            dma((chunks,)),
            dma((chunks,)),
            dma,
            dma((chunks,)),
            dma((chunks,)),
            dma,
            dma,
            dma,
        ],
        compiler_params=pltpu.CompilerParams(
            collective_id=0, has_side_effects=True, vmem_limit_bytes=60 * 2**20
        ),
    )(expert_ids, gate_weight, tokens, grad_mixed, w_gate, w_up, w_down)
    mixed, gtok, gg, gu, gd = pl.pallas_call(
        hand_over,
        out_shape=tuple(jax.ShapeDtypeStruct(o.shape, o.dtype) for o in outs),
        in_specs=[hbm] * 5,
        out_specs=(hbm,) * 5,
        scratch_shapes=[*(pltpu.VMEM(o.shape, o.dtype) for o in outs), dma((5,)), dma((5,))],
    )(*outs)
    return mixed, gtok, jnp.swapaxes(gg, 1, 2), jnp.swapaxes(gu, 1, 2), gd


def solution(mesh):
    both = P(("group", "hid"), None)
    return jax.shard_map(
        layer,
        mesh=mesh,
        in_specs=(
            both,
            both,
            both,
            both,
            P("hid", None, "ingroup"),
            P("hid", None, "ingroup"),
            P("hid", "ingroup", None),
        ),
        out_specs=(
            P(("group", "hid"), "ingroup"),
            P(("group", "hid"), "ingroup"),
            P("hid", "group", "ingroup"),
            P("hid", "group", "ingroup"),
            P("hid", "ingroup", "group"),
        ),
        check_vma=False,
    )
```

time: 98.4 us -> 83.9 us (0.85)
  local copies, waits for them, and re-layouts: 15.9 us -> 0 us
  Pallas kernels: 80.8 us -> 83 us
    unnamed x27 -> x0, local copies, waits for them, and re-layouts: 13.5 us -> none
    pallas_call x0 -> x1, Pallas kernels: none -> 2.56 us  [layer(): pl.pallas_call(hand_over, out_shape=tuple((jax.ShapeDtypeStruct(o.shape,...]
    pallas_call x2 -> x0, local copies, waits for them, and re-layouts: 2.34 us -> none  [layer(): pl.pallas_call(functools.partial(kernel, (n_g, n_j, n_h, chunks, depth, p...]
where the time goes in v2:
time: 83.9 us; the launch traced here: 83.6 us
  Pallas kernels  83 us (99%)
    pallas_call x1, Pallas kernels, layer(): pl.pallas_call(functools.partial(kernel, (n_g, n_j, n_h, chunks, depth, p...  80.4 us
    pallas_call x1, Pallas kernels, layer(): pl.pallas_call(hand_over, out_shape=tuple((jax.ShapeDtypeStruct(o.shape,...  2.56 us

profile of v2, /device:TPU:1, one launch (start us, length us, event | category | flops | bytes accessed | tf_op | source)
XLA Modules:
  0.0 83.6 jit_solution(10433677521170483283)
XLA Ops:
  0.6 80.4 %shard_map.110 = (bf16[16,256]{1,0:T(8,128)(2,1)}, bf16[16,256]{1,0:T(8,128)(2,1)}, f32[2,176,512]{2,1,0:T(8,128)}, f32[2,176,512]{2,1,0:T(8,128)}, f32[2,176,512]{2,1,0:T(8,128)}) custom-call(s32[6,16]{1,0:T(8,128)} %bitcast.8, f32[6,16]{1,0:T(8,128)} %bitcast.9, bf16[16,2048]{1,0:T(8,128)(2,1)} %tok_hbm.1, bf16[16,2048]{1,0:T(8,128)(2,1)} %grd_hbm.1, ...), custom_call_target="tpu_custom_call" | custom-call | tf_op jit(solution)/shard_map/pallas_call | solution.py:410
  81.0 2.6 %shard_map.111 = (bf16[16,256]{1,0:T(8,128)(2,1)}, bf16[16,256]{1,0:T(8,128)(2,1)}, f32[2,176,512]{2,1,0:T(8,128)}, f32[2,176,512]{2,1,0:T(8,128)}, f32[2,176,512]{2,1,0:T(8,128)}) custom-call(bf16[16,256]{1,0:T(8,128)(2,1)} %get-tuple-element.15.a, bf16[16,256]{1,0:T(8,128)(2,1)} %get-tuple-element.16.b, f32[2,176,512]{2,1,0:T(8,128)} %get-tuple-element.17.c, ...), custom_call_target="tpu_custom_call" | custom-call | tf_op jit(solution)/shard_map/pallas_call | solution.py:464

commit v3 on v2

--- a/solution.py
+++ b/solution.py
@@ -33,7 +33,7 @@
     ids, gw, tok, grd, wg, wu, wd, sel, unperm, perm,
     tile_s, tile_r, acts, part_s, twin_r, pair_s, part_r, back_s, back_r,
     xg_r, hr, mixed, gtok, og, ou, od,
-    in_sem, out_sem, send_sem, z_sem, y_sem, twin_sem, pair_sem, rs_sem, zb_sem, xg_sem, hr_sem,
+    in_sem, out_sem, send_sem, z_sem, y_sem, twin_sem, pair_sem, rs_sem, zb_sem, xg_sem, xt_sem, hr_sem,
 ):
     n_g, n_j, n_h, chunks, depth, per, top = dims
     rows = depth * CAP
@@ -198,7 +198,6 @@
 
         lax.fori_loop(1, n_y, body, 0)
 
-    before = None
     for c in (last, *range(last)):
         wait_recv(z_block(c, tile_r), z_sem.at[c])
         tiles = tile_r[c * depth : (c + 1) * depth].reshape(size, LANES)
@@ -215,28 +214,25 @@
 
         lax.fori_loop(1, n_y, forward, 0)
         to_twin(j, c)
-        if before is not None:
-            pass_on(before)
-        before = c
-    pass_on(before)
+    for c in (last, *range(last)):
+        pass_on(c)
     sent.append((acts.at[pl.ds(0, n_y - 1)], send_sem.at[1]))
     sent.append((acts.at[pl.ds(0, n_y)], send_sem.at[6]))
     for load in loads[4:]:
         load.wait()
     wait_recv(acts.at[pl.ds(0, n_y)], twin_sem)
 
-    wide = n_j // n_g
 
     def rows_out(o, carry):
         there = lax.rem(g + o, n_g)
         pltpu.make_async_remote_copy(
-            acts.at[pl.ds(there * wide, wide)], xg_r.at[g],
+            acts.at[2 * there + core], xg_r.at[g, core],
             send_sem.at[2], xg_sem, (there, j, h), MESH,
         ).start()
         return carry
 
     lax.fori_loop(1, n_g, rows_out, 0)
-    sent.append((xg_r.at[pl.ds(0, n_g - 1)], send_sem.at[2]))
+    sent.append((xg_r.at[pl.ds(0, n_g - 1), 0], send_sem.at[2]))
 
     m = chunks * rows
     units = wg.shape[1]
@@ -307,10 +303,8 @@
         lax.fori_loop(1, n_y, body, 0)
 
     for c in range(chunks):
-        if c == 0:
-            pair(0)
-        if c + 1 < chunks:
-            pair(c + 1)
+        pair(c)
+    for c in range(chunks):
         summed = part_s[j, c].astype(F32) + twin_r[y, c].astype(F32)
         wait_recv(part_r.at[:, c], rs_sem.at[c])
         for o in range(n_y - 1):
@@ -330,13 +324,25 @@
     sent.append((back_s.at[pl.ds(0, n_h - 1)], send_sem.at[5]))
     back_r[home] = back_s[home]
 
+    wait_recv(xg_r.at[pl.ds(0, n_g - 1), 0], xg_sem)
+
+    def rows_on(o, carry):
+        there = lax.rem(g + o, n_g)
+        pltpu.make_async_remote_copy(
+            xg_r.at[there, core], xg_r.at[there, core],
+            send_sem.at[8], xt_sem, twin, MESH,
+        ).start()
+        return carry
+
+    lax.fori_loop(1, n_g, rows_on, 0)
+    sent.append((xg_r.at[pl.ds(0, n_g - 1), 0], send_sem.at[8]))
+    xg_r[g] = acts[pl.ds(g * 2, 2)]
     wait_recv(hr.at[pl.ds(0, n_g - 1)], hr_sem)
-    wait_recv(xg_r.at[pl.ds(0, n_g - 1)], xg_sem)
-    xg_r[g] = acts[pl.ds(g * wide, wide)]
+    wait_recv(xg_r.at[pl.ds(0, n_g - 1), 0], xt_sem)
     for e in range(2):
         mine = slice(e * units, (e + 1) * units)
         ups = [hr[:, n, :, mine].reshape(n_g * m, units) for n in range(3)]
-        for b in range(wide):
+        for b in range(2):
             cols = slice(b * width, (b + 1) * width)
             x = xg_r[:, b, :, 0, e].reshape(n_g * m, width)
             gated = xg_r[:, b, :, 1, e].reshape(n_g * m, width)
@@ -401,7 +407,6 @@
     chunks = n_h // depth
     rows = depth * CAP
     width = 2 * LANES
-    wide = n_j // n_g
     m = chunks * rows
     share = d_model // n_g
     hbm = pl.BlockSpec(memory_space=pl.ANY)
@@ -438,7 +443,7 @@
             pltpu.VMEM((n_j // 2 - 1, *block), BF),
             pltpu.VMEM((n_h, 16, LANES), BF),
             pltpu.VMEM((n_h, 16, LANES), BF),
-            pltpu.VMEM((n_g, wide, *block), BF),
+            pltpu.VMEM((n_g, 2, *block), BF),
             pltpu.VMEM((n_g, 3, m, per * units), BF),
             pltpu.VMEM((toks, width), BF),
             pltpu.VMEM((toks, width), BF),
@@ -447,12 +452,13 @@
             pltpu.VMEM((per, units, share), F32),
             dma((7,)),
             dma((5,)),
-            dma((8,)),
+            dma((9,)),
             dma((chunks,)),
             dma((chunks,)),
             dma,
             dma((chunks,)),
             dma((chunks,)),
+            dma,
             dma,
             dma,
             dma,

time: 83.9 us -> 80.5 us (0.959)
  the two profiles are of different devices: /device:TPU:1 before, /device:TPU:36 now
where the time goes in v3:
time: 80.5 us; the launch traced here: 80.3 us
  Pallas kernels  79.6 us (99%)
    pallas_call x1, Pallas kernels, layer(): pl.pallas_call(functools.partial(kernel, (n_g, n_j, n_h, chunks, depth, p...  77.1 us
    pallas_call x1, Pallas kernels, layer(): pl.pallas_call(hand_over, out_shape=tuple((jax.ShapeDtypeStruct(o.shape,...  2.56 us

profile of v3, /device:TPU:36, one launch (start us, length us, event | category | flops | bytes accessed | tf_op | source)
XLA Modules:
  0.0 80.3 jit_solution(8317870111757725468)
XLA Ops:
  0.6 77.1 %shard_map.110 = (bf16[16,256]{1,0:T(8,128)(2,1)}, bf16[16,256]{1,0:T(8,128)(2,1)}, f32[2,176,512]{2,1,0:T(8,128)}, f32[2,176,512]{2,1,0:T(8,128)}, f32[2,176,512]{2,1,0:T(8,128)}) custom-call(s32[6,16]{1,0:T(8,128)} %bitcast.8, f32[6,16]{1,0:T(8,128)} %bitcast.9, bf16[16,2048]{1,0:T(8,128)(2,1)} %tok_hbm.1, bf16[16,2048]{1,0:T(8,128)(2,1)} %grd_hbm.1, ...), custom_call_target="tpu_custom_call" | custom-call | tf_op jit(solution)/shard_map/pallas_call | solution.py:415
  77.7 2.6 %shard_map.111 = (bf16[16,256]{1,0:T(8,128)(2,1)}, bf16[16,256]{1,0:T(8,128)(2,1)}, f32[2,176,512]{2,1,0:T(8,128)}, f32[2,176,512]{2,1,0:T(8,128)}, f32[2,176,512]{2,1,0:T(8,128)}) custom-call(bf16[16,256]{1,0:T(8,128)(2,1)} %get-tuple-element.15.a, bf16[16,256]{1,0:T(8,128)(2,1)} %get-tuple-element.16.b, f32[2,176,512]{2,1,0:T(8,128)} %get-tuple-element.17.c, ...), custom_call_target="tpu_custom_call" | custom-call | tf_op jit(solution)/shard_map/pallas_call | solution.py:470

commit v4 on v3

--- a/solution.py
+++ b/solution.py
@@ -31,9 +31,9 @@
     ids_hbm, gw_hbm, tok_hbm, grd_hbm, wg_hbm, wu_hbm, wd_hbm,
     mixed_hbm, gtok_hbm, gg_hbm, gu_hbm, gd_hbm,
     ids, gw, tok, grd, wg, wu, wd, sel, unperm, perm,
-    tile_s, tile_r, acts, part_s, twin_r, pair_s, part_r, back_s, back_r,
+    tile_s, tile_r, relay, acts, part_s, twin_r, pair_s, part_r, back_s, back_r,
     xg_r, hr, mixed, gtok, og, ou, od,
-    in_sem, out_sem, send_sem, z_sem, y_sem, twin_sem, pair_sem, rs_sem, zb_sem, xg_sem, xt_sem, hr_sem,
+    in_sem, out_sem, send_sem, relay_sem, z_sem, y_sem, twin_sem, pair_sem, rs_sem, zb_sem, xg_sem, xt_sem, hr_sem,
 ):
     n_g, n_j, n_h, chunks, depth, per, top = dims
     rows = depth * CAP
@@ -87,7 +87,8 @@
     def group_peer(o):
         return (lax.rem(g + o, n_g), j, h)
 
-    greet(n_h, hid_peer)
+    greet(n_h // 4 + 1, hid_peer)
+    greet(n_h // 4 + 1, lambda o: hid_peer(n_h - o))
     greet(n_y, y_peer)
     pl.semaphore_signal(barrier, inc=1, device_id=twin, device_id_type=MESH)
     greet(n_g, group_peer)
@@ -150,7 +151,7 @@
     home = (chunks - 1) * depth
     tile_r[home] = tile_s[home]
 
-    pl.semaphore_wait(barrier, n_h - 1 + n_y - 1 + 1 + n_g - 1)
+    pl.semaphore_wait(barrier, n_h // 4 * 2 + n_y - 1 + 1 + n_g - 1)
 
     def wait_recv(ref, sem):
         pltpu.make_async_remote_copy(ref, ref, sem, sem, twin, MESH).wait_recv()
@@ -176,13 +177,45 @@
         lax.fori_loop(1 if c == chunks - 1 else 0, depth, body, 0)
 
     def z_block(c, ref):
-        return ref.at[pl.ds(c * depth + (c == chunks - 1), depth - (c == chunks - 1))]
-
-    last = chunks - 1
-    order = [*range(last - 1), last, last - 1]
-    for c in order:
+        own = c in (chunks // 2 - 1, chunks - 1)
+        return ref.at[pl.ds(c * depth + own, depth - own)]
+
+    reach, last = n_h // 4, chunks - 1
+    outer = chunks // 2
+
+    def side(c, up):
+        return pl.ds(c * depth + (0 if up else half), half)
+
+    def via(up):
+        return (g, j, lax.rem(h + (reach if up else n_h - reach), n_h))
+
+    for c in range(outer):
+        for up in (True, False):
+            pltpu.make_async_remote_copy(
+                tile_s.at[side(c, up)], relay.at[side(c, up)],
+                send_sem.at[0], relay_sem.at[2 * c + (not up)], via(up), MESH,
+            ).start()
+    for c in range(last, outer - 1, -1):
         z_send(c, tile_s, tile_r, 1, send_sem.at[0], z_sem.at[c])
     sent.append((tile_s.at[pl.ds(0, n_h - 1)], send_sem.at[0]))
+    for c in range(outer):
+        for up in (True, False):
+            wait_recv(relay.at[side(c, up)], relay_sem.at[2 * c + (not up)])
+
+            def onward(t, carry, c=c, up=up):
+                at = c * depth + t + (0 if up else half)
+                away = half * (outer - 1 - c) + t if up else n_h - reach + half * c + t
+                pltpu.make_async_remote_copy(
+                    relay.at[at], tile_r.at[at], send_sem.at[9], z_sem.at[c],
+                    (g, j, lax.rem(h + away, n_h)), MESH,
+                ).start()
+                return carry
+
+            mine = up and c == outer - 1
+            lax.fori_loop(1 if mine else 0, half, onward, 0)
+            if mine:
+                tile_r[c * depth] = relay[c * depth]
+    sent.append((relay.at[pl.ds(0, n_h // 2 - 1)], send_sem.at[9]))
 
     def to_twin(b, c):
         pltpu.make_async_remote_copy(
@@ -198,7 +231,8 @@
 
         lax.fori_loop(1, n_y, body, 0)
 
-    for c in (last, *range(last)):
+    order = [*range(last, outer - 1, -1), *range(outer)]
+    for c in order:
         wait_recv(z_block(c, tile_r), z_sem.at[c])
         tiles = tile_r[c * depth : (c + 1) * depth].reshape(size, LANES)
         ordered = dot(unperm[...], tiles).astype(BF)
@@ -214,7 +248,7 @@
 
         lax.fori_loop(1, n_y, forward, 0)
         to_twin(j, c)
-    for c in (last, *range(last)):
+    for c in order:
         pass_on(c)
     sent.append((acts.at[pl.ds(0, n_y - 1)], send_sem.at[1]))
     sent.append((acts.at[pl.ds(0, n_y)], send_sem.at[6]))
@@ -436,6 +470,7 @@
             pltpu.VMEM((depth * 16, depth * 16), BF),
             pltpu.VMEM((n_h, 16, LANES), BF),
             pltpu.VMEM((n_h, 16, LANES), BF),
+            pltpu.VMEM((n_h // 2, 16, LANES), BF),
             pltpu.VMEM((n_j, *block), BF),
             pltpu.VMEM((n_j, *block), BF),
             pltpu.VMEM((n_j // 2, *block), BF),
@@ -452,7 +487,8 @@
             pltpu.VMEM((per, units, share), F32),
             dma((7,)),
             dma((5,)),
-            dma((9,)),
+            dma((10,)),
+            dma((chunks,)),
             dma((chunks,)),
             dma((chunks,)),
             dma,

time: 80.5 us -> 76.5 us (0.950)
  the two profiles are of different devices: /device:TPU:36 before, /device:TPU:22 now
where the time goes in v4:
time: 76.5 us; the launch traced here: 76.3 us
  Pallas kernels  75.6 us (99%)
    pallas_call x1, Pallas kernels, layer(): pl.pallas_call(functools.partial(kernel, (n_g, n_j, n_h, chunks, depth, p...  73.1 us
    pallas_call x1, Pallas kernels, layer(): pl.pallas_call(hand_over, out_shape=tuple((jax.ShapeDtypeStruct(o.shape,...  2.56 us

profile of v4, /device:TPU:22, one launch (start us, length us, event | category | flops | bytes accessed | tf_op | source)
XLA Modules:
  0.0 76.3 jit_solution(4850887727675899290)
XLA Ops:
  0.6 73.1 %shard_map.110 = (bf16[16,256]{1,0:T(8,128)(2,1)}, bf16[16,256]{1,0:T(8,128)(2,1)}, f32[2,176,512]{2,1,0:T(8,128)}, f32[2,176,512]{2,1,0:T(8,128)}, f32[2,176,512]{2,1,0:T(8,128)}) custom-call(s32[6,16]{1,0:T(8,128)} %bitcast.8, f32[6,16]{1,0:T(8,128)} %bitcast.9, bf16[16,2048]{1,0:T(8,128)(2,1)} %tok_hbm.1, bf16[16,2048]{1,0:T(8,128)(2,1)} %grd_hbm.1, ...), custom_call_target="tpu_custom_call" | custom-call | tf_op jit(solution)/shard_map/pallas_call | solution.py:449
  73.7 2.6 %shard_map.111 = (bf16[16,256]{1,0:T(8,128)(2,1)}, bf16[16,256]{1,0:T(8,128)(2,1)}, f32[2,176,512]{2,1,0:T(8,128)}, f32[2,176,512]{2,1,0:T(8,128)}, f32[2,176,512]{2,1,0:T(8,128)}) custom-call(bf16[16,256]{1,0:T(8,128)(2,1)} %get-tuple-element.15.a, bf16[16,256]{1,0:T(8,128)(2,1)} %get-tuple-element.16.b, f32[2,176,512]{2,1,0:T(8,128)} %get-tuple-element.17.c, ...), custom_call_target="tpu_custom_call" | custom-call | tf_op jit(solution)/shard_map/pallas_call | solution.py:506

commit v5 on v4

--- a/solution.py
+++ b/solution.py
@@ -198,6 +198,39 @@
     for c in range(last, outer - 1, -1):
         z_send(c, tile_s, tile_r, 1, send_sem.at[0], z_sem.at[c])
     sent.append((tile_s.at[pl.ds(0, n_h - 1)], send_sem.at[0]))
+    def to_twin(b, c):
+        pltpu.make_async_remote_copy(
+            acts.at[b, c], acts.at[b, c], send_sem.at[6], twin_sem, twin, MESH
+        ).start()
+
+    def pass_on(c):
+        wait_recv(acts.at[pl.ds(0, n_y - 1), c], y_sem.at[c])
+
+        def body(o, carry):
+            to_twin(2 * y_at(o) + core, c)
+            return carry
+
+        lax.fori_loop(1, n_y, body, 0)
+
+    order = [*range(last, outer - 1, -1), *range(outer)]
+    def take(c):
+        wait_recv(z_block(c, tile_r), z_sem.at[c])
+        tiles = tile_r[c * depth : (c + 1) * depth].reshape(size, LANES)
+        ordered = dot(unperm[...], tiles).astype(BF)
+        acts[j, c, :, :, :, :LANES] = ordered[: size // 2].reshape(2, 2, rows, LANES)
+        acts[j, c, :, :, :, LANES:] = ordered[size // 2 :].reshape(2, 2, rows, LANES)
+
+        def forward(o, carry, c=c):
+            pltpu.make_async_remote_copy(
+                acts.at[j, c], acts.at[j, c],
+                send_sem.at[1], y_sem.at[c], y_peer(o), MESH,
+            ).start()
+            return carry
+
+        lax.fori_loop(1, n_y, forward, 0)
+        to_twin(j, c)
+
+    take(last)
     for c in range(outer):
         for up in (True, False):
             wait_recv(relay.at[side(c, up)], relay_sem.at[2 * c + (not up)])
@@ -216,38 +249,8 @@
             if mine:
                 tile_r[c * depth] = relay[c * depth]
     sent.append((relay.at[pl.ds(0, n_h // 2 - 1)], send_sem.at[9]))
-
-    def to_twin(b, c):
-        pltpu.make_async_remote_copy(
-            acts.at[b, c], acts.at[b, c], send_sem.at[6], twin_sem, twin, MESH
-        ).start()
-
-    def pass_on(c):
-        wait_recv(acts.at[pl.ds(0, n_y - 1), c], y_sem.at[c])
-
-        def body(o, carry):
-            to_twin(2 * y_at(o) + core, c)
-            return carry
-
-        lax.fori_loop(1, n_y, body, 0)
-
-    order = [*range(last, outer - 1, -1), *range(outer)]
-    for c in order:
-        wait_recv(z_block(c, tile_r), z_sem.at[c])
-        tiles = tile_r[c * depth : (c + 1) * depth].reshape(size, LANES)
-        ordered = dot(unperm[...], tiles).astype(BF)
-        acts[j, c, :, :, :, :LANES] = ordered[: size // 2].reshape(2, 2, rows, LANES)
-        acts[j, c, :, :, :, LANES:] = ordered[size // 2 :].reshape(2, 2, rows, LANES)
-
-        def forward(o, carry, c=c):
-            pltpu.make_async_remote_copy(
-                acts.at[j, c], acts.at[j, c],
-                send_sem.at[1], y_sem.at[c], y_peer(o), MESH,
-            ).start()
-            return carry
-
-        lax.fori_loop(1, n_y, forward, 0)
-        to_twin(j, c)
+    for c in order[1:]:
+        take(c)
     for c in order:
         pass_on(c)
     sent.append((acts.at[pl.ds(0, n_y - 1)], send_sem.at[1]))

time: 76.5 us -> 77.4 us (1.012)
  the two profiles are of different devices: /device:TPU:22 before, /device:TPU:32 now
where the time goes in v5:
time: 77.4 us; the launch traced here: 77.2 us
  Pallas kernels  76.6 us (99%)
    pallas_call x1, Pallas kernels, layer(): pl.pallas_call(functools.partial(kernel, (n_g, n_j, n_h, chunks, depth, p...  74 us
    pallas_call x1, Pallas kernels, layer(): pl.pallas_call(hand_over, out_shape=tuple((jax.ShapeDtypeStruct(o.shape,...  2.56 us

profile of v5, /device:TPU:32, one launch (start us, length us, event | category | flops | bytes accessed | tf_op | source)
XLA Modules:
  0.0 77.2 jit_solution(15279189813262291125)
XLA Ops:
  0.6 74.0 %shard_map.110 = (bf16[16,256]{1,0:T(8,128)(2,1)}, bf16[16,256]{1,0:T(8,128)(2,1)}, f32[2,176,512]{2,1,0:T(8,128)}, f32[2,176,512]{2,1,0:T(8,128)}, f32[2,176,512]{2,1,0:T(8,128)}) custom-call(s32[6,16]{1,0:T(8,128)} %bitcast.8, f32[6,16]{1,0:T(8,128)} %bitcast.9, bf16[16,2048]{1,0:T(8,128)(2,1)} %tok_hbm.1, bf16[16,2048]{1,0:T(8,128)(2,1)} %grd_hbm.1, ...), custom_call_target="tpu_custom_call" | custom-call | tf_op jit(solution)/shard_map/pallas_call | solution.py:452
  74.7 2.6 %shard_map.111 = (bf16[16,256]{1,0:T(8,128)(2,1)}, bf16[16,256]{1,0:T(8,128)(2,1)}, f32[2,176,512]{2,1,0:T(8,128)}, f32[2,176,512]{2,1,0:T(8,128)}, f32[2,176,512]{2,1,0:T(8,128)}) custom-call(bf16[16,256]{1,0:T(8,128)(2,1)} %get-tuple-element.15.a, bf16[16,256]{1,0:T(8,128)(2,1)} %get-tuple-element.16.b, f32[2,176,512]{2,1,0:T(8,128)} %get-tuple-element.17.c, ...), custom_call_target="tpu_custom_call" | custom-call | tf_op jit(solution)/shard_map/pallas_call | solution.py:509
